TPU v7x, 512 devices: a whole 4x8x8 slice. The times are simulated.
512 devices in a mesh: leaf: 512 (over y, x, z, core).
Axes of the slice: x: 4, y: 8, z: 8, core: 2. Of those that a mesh axis runs over, the one named last changes fastest.
Arguments:
- features: bfloat16 [262144, 128], P('leaf'), may hold values from -0.75 to 0.75
- noise: float32 [262144], P('leaf'), may hold values from 0.5 to 2
- targets: float32 [262144, 128], P('leaf'), may hold values from -6 to 6
- anchors: bfloat16 [3, 2, 128, 128], replicated, may hold values from -0.75 to 0.75
- order: int32 [262144], P('leaf'), may hold values from 0 to 262143, as said below
Outputs:
- solved: float32 [262144, 128], P('leaf')
- coupling: float32 [3, 131072, 128], P(None, 'leaf')
Inputs may be any that keep to these rules, and one draw needn't show every extreme that they name: `order`: each aligned block of 512 entries is a permutation of that block's own indices.
All inputs are finite; a program needn't handle non-finite values.
Results may differ from a plain program's by a relative error of at most 0.0003.
Values sent between devices are 32-bit elements; how exact they have to be, the bound alone decides.
No kernel may reach another device: no remote copies, remote signals or barrier semaphores. Data moves between devices by JAX's collectives and lax.ppermute only.
A program may use at most 64 MiB of HBM per device.

v0:
```python
import math

import jax
import jax.numpy as jnp
from jax import lax
from jax.sharding import PartitionSpec as P

length_scale = 0.5
kernel_gain = 64.0


def partner(value, axis, bit):
    mask = 2**bit
    pairs = [(source, source ^ mask) for source in range(lax.axis_size(axis))]
    return lax.ppermute(value, axis, pairs)


def kernel_panel(points, anchor_set, weight):
    cross = jnp.dot(points, anchor_set.T, preferred_element_type=jnp.float32)
    point_norm = jnp.sum(points.astype(jnp.float32) ** 2, axis=1, keepdims=True)
    anchor_norm = jnp.sum(anchor_set.astype(jnp.float32) ** 2, axis=1)[None, :]
    distance = jnp.sqrt(point_norm + anchor_norm - 2.0 * cross)
    scaled = math.sqrt(3.0) * distance / length_scale
    return weight * (1.0 + scaled) * jnp.exp(-scaled)


def group_total(term, bit):
    steps = list(range(bit + 1))
    for step in steps:
        term = term + partner(term, "leaf", step)
    return term


def on_device(features, noise, targets, anchors, order):
    count = features.shape[0]
    leaves = lax.axis_size("leaf")
    top = leaves.bit_length() - 1
    levels = anchors.shape[0]
    rank = anchors.shape[2]
    width = 2 * rank
    nrhs = targets.shape[1]
    device = lax.axis_index("leaf")
    local = order - device * count
    points = jnp.take(features, local, axis=0)
    inverse = 1.0 / jnp.take(noise, local, axis=0)
    rhs = jnp.take(targets, local, axis=0)
    panels = []
    for level in range(levels):
        bit = top - levels + level
        side = device >> bit & 1
        own_set = jnp.where(side == 0, anchors[level, 0], anchors[level, 1])
        other_set = jnp.where(side == 0, anchors[level, 1], anchors[level, 0])
        weight = kernel_gain / math.sqrt(count * 2 ** (bit + 1))
        panels.append(kernel_panel(points, jnp.concatenate([own_set, other_set], axis=0), weight))
    states = [panel * inverse[:, None] for panel in panels]
    solved = rhs * inverse[:, None]
    coefs = []
    for level in range(levels):
        bit = top - levels + level
        stack = jnp.concatenate(states[level:] + [solved], axis=1)
        term = lax.dot_general(
            panels[level],
            stack,
            (((0,), (0,)), ((), ())),
            precision=lax.Precision.HIGHEST,
            preferred_element_type=jnp.float32,
        )
        total = group_total(term, bit)
        core = jnp.eye(width, dtype=jnp.float32) + total[:, :width]
        factor = jnp.linalg.cholesky(core)
        mixed = jax.scipy.linalg.cho_solve((factor, True), total[:, width:])
        update = jnp.dot(
            states[level],
            mixed,
            precision=lax.Precision.HIGHEST,
            preferred_element_type=jnp.float32,
        )
        for later in range(level + 1, levels):
            start = (later - level - 1) * width
            states[later] = states[later] - update[:, start : start + width]
        solved = solved - update[:, -nrhs:]
        coefs.append(mixed[:, -nrhs:])
    return (solved, jnp.stack(coefs))


def solution(mesh):
    in_specs = (P("leaf", None), P("leaf"), P("leaf", None), P(), P("leaf"))
    out_specs = (P("leaf", None), P(None, "leaf", None))
    return jax.shard_map(
        on_device, mesh=mesh, in_specs=in_specs, out_specs=out_specs, check_vma=False
    )
```

profile of v0, /device:TPU:1, one launch (start us, length us, event | category | flops | bytes accessed | tf_op | source)
XLA Modules:
  0.0 734.5 jit_solution(10050012525999526490)
XLA Ops:
  1.5 3.5 gather_fusion.1
  9.5 1.7 fusion
  11.2 8.8 %collective-permute-start = (f32[256,896]{0,1:T(8,128)S(1)}, f32[256,896]{0,1:T(8,128)S(1)}, u32[]{:S(2)}, u32[]{:S(2)}) collective-permute-start(f32[256,896]{0,1:T(8,128)S(1)} %fusion), channel_id=1, source_target_pairs={{0,1},{1,0},{2,3},{3,2},{4,5},{5,4},{6,7},{7,6},{8,9},{9,8},{10,11... | collective-permute-start | bytes 2752520 | tf_op jit(solution)/shard_map/ppermute | solution.py:15
  20.0 2.1 collective-permute-done
  22.2 1.9 collective-permute-start.1
  24.1 21.5 %collective-permute-done.1 = f32[256,896]{0,1:T(8,128)S(1)} collective-permute-done((f32[256,896]{0,1:T(8,128)S(1)}, f32[256,896]{0,1:T(8,128)S(1)}, u32[]{:S(2)}, u32[]{:S(2)}) %collective-permute-start.1) | collective-permute-done | bytes 917536 | tf_op jit(solution)/shard_map/ppermute | solution.py:15
  45.8 1.9 collective-permute-start.2
  47.7 42.7 %collective-permute-done.2 = f32[256,896]{0,1:T(8,128)S(1)} collective-permute-done((f32[256,896]{0,1:T(8,128)S(1)}, f32[256,896]{0,1:T(8,128)S(1)}, u32[]{:S(2)}, u32[]{:S(2)}) %collective-permute-start.2) | collective-permute-done | bytes 917536 | tf_op jit(solution)/shard_map/ppermute | solution.py:15
  90.6 4.3 collective-permute-start.3
  94.9 42.7 %collective-permute-done.3 = f32[256,896]{0,1:T(8,128)S(1)} collective-permute-done((f32[256,896]{0,1:T(8,128)S(1)}, f32[256,896]{0,1:T(8,128)S(1)}, u32[]{:S(2)}, u32[]{:S(2)}) %collective-permute-start.3) | collective-permute-done | bytes 917536 | tf_op jit(solution)/shard_map/ppermute | solution.py:15
  137.8 1.9 collective-permute-start.4
  139.7 21.4 %collective-permute-done.4 = f32[256,896]{0,1:T(8,128)S(1)} collective-permute-done((f32[256,896]{0,1:T(8,128)S(1)}, f32[256,896]{0,1:T(8,128)S(1)}, u32[]{:S(2)}, u32[]{:S(2)}) %collective-permute-start.4) | collective-permute-done | bytes 917536 | tf_op jit(solution)/shard_map/ppermute | solution.py:15
  161.2 1.9 collective-permute-start.5
  163.1 22.0 %collective-permute-done.5 = f32[256,896]{0,1:T(8,128)S(1)} collective-permute-done((f32[256,896]{0,1:T(8,128)S(1)}, f32[256,896]{0,1:T(8,128)S(1)}, u32[]{:S(2)}, u32[]{:S(2)}) %collective-permute-start.5) | collective-permute-done | bytes 917536 | tf_op jit(solution)/shard_map/ppermute | solution.py:15
  185.2 2.1 collective-permute-start.6
  187.4 19.4 %collective-permute-done.6 = f32[256,896]{0,1:T(8,128)} collective-permute-done((f32[256,896]{0,1:T(8,128)S(1)}, f32[256,896]{0,1:T(8,128)}, u32[]{:S(2)}, u32[]{:S(2)}) %collective-permute-start.6) | collective-permute-done | bytes 917536 | tf_op jit(solution)/shard_map/ppermute | solution.py:15
  208.3 11.7 %cholesky.172 = f32[128,128]{1,0:T(8,128)S(1)} custom-call(f32[128,128]{1,0:T(8,128)S(1)} %cholesky.270), custom_call_target="Cholesky" | custom-call | tf_op jit(solution)/shard_map/jit(cholesky)/cholesky | solution.py:70
  220.1 9.8 %custom-call.34 = f32[1,128,128]{1,2,0:T(8,128)S(1)} custom-call(f32[1,128,128]{2,1,0:T(8,128)S(1)} %get-tuple-element.82), custom_call_target="InvertDiagBlocksLowerTriangular" | custom-call | tf_op jit(solution)/shard_map/jit(cholesky)/cholesky | solution.py:70
  230.4 11.7 %cholesky.189 = f32[128,128]{1,0:T(8,128)S(1)} custom-call(f32[128,128]{1,0:T(8,128)S(1)} %convolution_subtract_fusion.6), custom_call_target="Cholesky" | custom-call | tf_op jit(solution)/shard_map/jit(cholesky)/cholesky | solution.py:70
  244.9 4.4 while.3
  249.3 19.7 %custom-call.29 = f32[2,128,128]{1,2,0:T(8,128)S(1)} custom-call(f32[2,128,128]{2,1,0:T(8,128)S(1)} %get-tuple-element.10), custom_call_target="InvertDiagBlocksLowerTriangular" | custom-call | tf_op jit(solution)/shard_map/jit(_cho_solve)/triangular_solve | solution.py:71
  275.6 5.1 collective-permute-start.7
  280.7 1.7 collective-permute-done.7
  282.5 1.9 collective-permute-start.8
  284.4 15.9 %collective-permute-done.8 = f32[256,640]{0,1:T(8,128)S(1)} collective-permute-done((f32[256,640]{0,1:T(8,128)S(1)}, f32[256,640]{0,1:T(8,128)S(1)}, u32[]{:S(2)}, u32[]{:S(2)}) %collective-permute-start.8) | collective-permute-done | bytes 655392 | tf_op jit(solution)/shard_map/ppermute | solution.py:15
  300.4 1.9 collective-permute-start.9
  302.3 31.5 %collective-permute-done.9 = f32[256,640]{0,1:T(8,128)S(1)} collective-permute-done((f32[256,640]{0,1:T(8,128)S(1)}, f32[256,640]{0,1:T(8,128)S(1)}, u32[]{:S(2)}, u32[]{:S(2)}) %collective-permute-start.9) | collective-permute-done | bytes 655392 | tf_op jit(solution)/shard_map/ppermute | solution.py:15
  333.9 4.9 collective-permute-start.10
  338.8 31.5 %collective-permute-done.10 = f32[256,640]{0,1:T(8,128)S(1)} collective-permute-done((f32[256,640]{0,1:T(8,128)S(1)}, f32[256,640]{0,1:T(8,128)S(1)}, u32[]{:S(2)}, u32[]{:S(2)}) %collective-permute-start.10) | collective-permute-done | bytes 655392 | tf_op jit(solution)/shard_map/ppermute | solution.py:15
  370.4 2.6 collective-permute-start.11
  372.9 15.1 %collective-permute-done.11 = f32[256,640]{0,1:T(8,128)S(1)} collective-permute-done((f32[256,640]{0,1:T(8,128)S(1)}, f32[256,640]{0,1:T(8,128)S(1)}, u32[]{:S(2)}, u32[]{:S(2)}) %collective-permute-start.11) | collective-permute-done | bytes 655392 | tf_op jit(solution)/shard_map/ppermute | solution.py:15
  388.1 2.2 collective-permute-start.12
  390.4 16.1 %collective-permute-done.12 = f32[256,640]{0,1:T(8,128)S(1)} collective-permute-done((f32[256,640]{0,1:T(8,128)S(1)}, f32[256,640]{0,1:T(8,128)S(1)}, u32[]{:S(2)}, u32[]{:S(2)}) %collective-permute-start.12) | collective-permute-done | bytes 655392 | tf_op jit(solution)/shard_map/ppermute | solution.py:15
  406.5 1.9 collective-permute-start.13
  408.4 13.9 %collective-permute-done.13 = f32[256,640]{0,1:T(8,128)S(1)} collective-permute-done((f32[256,640]{0,1:T(8,128)S(1)}, f32[256,640]{0,1:T(8,128)S(1)}, u32[]{:S(2)}, u32[]{:S(2)}) %collective-permute-start.13) | collective-permute-done | bytes 655392 | tf_op jit(solution)/shard_map/ppermute | solution.py:15
  422.5 2.1 collective-permute-start.14
  424.6 31.2 %collective-permute-done.14 = f32[256,640]{0,1:T(8,128)} collective-permute-done((f32[256,640]{0,1:T(8,128)S(1)}, f32[256,640]{0,1:T(8,128)}, u32[]{:S(2)}, u32[]{:S(2)}) %collective-permute-start.14) | collective-permute-done | bytes 655392 | tf_op jit(solution)/shard_map/ppermute | solution.py:15
  458.7 11.7 %cholesky.206 = f32[128,128]{1,0:T(8,128)S(1)} custom-call(f32[128,128]{1,0:T(8,128)S(1)} %cholesky.273), custom_call_target="Cholesky" | custom-call | tf_op jit(solution)/shard_map/jit(cholesky)/cholesky | solution.py:70
  470.5 9.8 %custom-call.35 = f32[1,128,128]{1,2,0:T(8,128)S(1)} custom-call(f32[1,128,128]{2,1,0:T(8,128)S(1)} %get-tuple-element.78), custom_call_target="InvertDiagBlocksLowerTriangular" | custom-call | tf_op jit(solution)/shard_map/jit(cholesky)/cholesky | solution.py:70
  482.5 11.7 %cholesky.223 = f32[128,128]{1,0:T(8,128)S(1)} custom-call(f32[128,128]{1,0:T(8,128)S(1)} %convolution_subtract_fusion.5), custom_call_target="Cholesky" | custom-call | tf_op jit(solution)/shard_map/jit(cholesky)/cholesky | solution.py:70
  496.8 4.1 while.4
  501.0 19.7 %custom-call.30 = f32[2,128,128]{1,2,0:T(8,128)S(1)} custom-call(f32[2,128,128]{2,1,0:T(8,128)S(1)} %get-tuple-element.18), custom_call_target="InvertDiagBlocksLowerTriangular" | custom-call | tf_op jit(solution)/shard_map/jit(_cho_solve)/triangular_solve | solution.py:71
  527.7 2.4 collective-permute-start.15
  531.5 1.9 collective-permute-start.16
  533.5 10.3 %collective-permute-done.16 = f32[256,384]{0,1:T(8,128)S(1)} collective-permute-done((f32[256,384]{0,1:T(8,128)S(1)}, f32[256,384]{0,1:T(8,128)S(1)}, u32[]{:S(2)}, u32[]{:S(2)}) %collective-permute-start.16) | collective-permute-done | bytes 393248 | tf_op jit(solution)/shard_map/ppermute | solution.py:15
  543.8 1.9 collective-permute-start.17
  545.7 20.3 %collective-permute-done.17 = f32[256,384]{0,1:T(8,128)S(1)} collective-permute-done((f32[256,384]{0,1:T(8,128)S(1)}, f32[256,384]{0,1:T(8,128)S(1)}, u32[]{:S(2)}, u32[]{:S(2)}) %collective-permute-start.17) | collective-permute-done | bytes 393248 | tf_op jit(solution)/shard_map/ppermute | solution.py:15
  566.1 4.3 collective-permute-start.18
  570.4 20.2 %collective-permute-done.18 = f32[256,384]{0,1:T(8,128)S(1)} collective-permute-done((f32[256,384]{0,1:T(8,128)S(1)}, f32[256,384]{0,1:T(8,128)S(1)}, u32[]{:S(2)}, u32[]{:S(2)}) %collective-permute-start.18) | collective-permute-done | bytes 393248 | tf_op jit(solution)/shard_map/ppermute | solution.py:15
  590.7 2.6 collective-permute-start.19
  593.3 9.5 %collective-permute-done.19 = f32[256,384]{0,1:T(8,128)S(1)} collective-permute-done((f32[256,384]{0,1:T(8,128)S(1)}, f32[256,384]{0,1:T(8,128)S(1)}, u32[]{:S(2)}, u32[]{:S(2)}) %collective-permute-start.19) | collective-permute-done | bytes 393248 | tf_op jit(solution)/shard_map/ppermute | solution.py:15
  602.8 2.4 collective-permute-start.20
  605.2 10.3 %collective-permute-done.20 = f32[256,384]{0,1:T(8,128)S(1)} collective-permute-done((f32[256,384]{0,1:T(8,128)S(1)}, f32[256,384]{0,1:T(8,128)S(1)}, u32[]{:S(2)}, u32[]{:S(2)}) %collective-permute-start.20) | collective-permute-done | bytes 393248 | tf_op jit(solution)/shard_map/ppermute | solution.py:15
  615.6 1.9 collective-permute-start.21
  617.5 8.3 %collective-permute-done.21 = f32[256,384]{0,1:T(8,128)S(1)} collective-permute-done((f32[256,384]{0,1:T(8,128)S(1)}, f32[256,384]{0,1:T(8,128)S(1)}, u32[]{:S(2)}, u32[]{:S(2)}) %collective-permute-start.21) | collective-permute-done | bytes 393248 | tf_op jit(solution)/shard_map/ppermute | solution.py:15
  625.9 1.9 collective-permute-start.22
  627.8 20.3 %collective-permute-done.22 = f32[256,384]{0,1:T(8,128)S(1)} collective-permute-done((f32[256,384]{0,1:T(8,128)S(1)}, f32[256,384]{0,1:T(8,128)S(1)}, u32[]{:S(2)}, u32[]{:S(2)}) %collective-permute-start.22) | collective-permute-done | bytes 393248 | tf_op jit(solution)/shard_map/ppermute | solution.py:15
  648.2 2.2 collective-permute-start.23
  650.4 19.3 %collective-permute-done.23 = f32[256,384]{0,1:T(8,128)S(1)} collective-permute-done((f32[256,384]{0,1:T(8,128)S(1)}, f32[256,384]{0,1:T(8,128)S(1)}, u32[]{:S(2)}, u32[]{:S(2)}) %collective-permute-start.23) | collective-permute-done | bytes 393248 | tf_op jit(solution)/shard_map/ppermute | solution.py:15
  669.9 11.7 %cholesky.240 = f32[128,128]{1,0:T(8,128)S(1)} custom-call(f32[128,128]{1,0:T(8,128)S(1)} %cholesky.276), custom_call_target="Cholesky" | custom-call | tf_op jit(solution)/shard_map/jit(cholesky)/cholesky | solution.py:70
  681.7 9.8 %custom-call.36 = f32[1,128,128]{1,2,0:T(8,128)S(1)} custom-call(f32[1,128,128]{2,1,0:T(8,128)S(1)} %get-tuple-element.74), custom_call_target="InvertDiagBlocksLowerTriangular" | custom-call | tf_op jit(solution)/shard_map/jit(cholesky)/cholesky | solution.py:70
  692.0 11.7 %cholesky.257 = f32[128,128]{1,0:T(8,128)S(1)} custom-call(f32[128,128]{1,0:T(8,128)S(1)} %convolution_subtract_fusion.4), custom_call_target="Cholesky" | custom-call | tf_op jit(solution)/shard_map/jit(cholesky)/cholesky | solution.py:70
  706.4 4.3 while.5
  710.7 19.7 %custom-call.31 = f32[2,128,128]{1,2,0:T(8,128)S(1)} custom-call(f32[2,128,128]{2,1,0:T(8,128)S(1)} %get-tuple-element.26), custom_call_target="InvertDiagBlocksLowerTriangular" | custom-call | tf_op jit(solution)/shard_map/jit(_cho_solve)/triangular_solve | solution.py:71
  (164 shorter events, 49.2 us)
Async XLA Ops:
  0.6 5.8 copy-start
  0.6 4.3 copy-start.16
  0.7 0.8 copy-start.1
  0.7 4.3 copy-start.2
  6.5 1.2 copy-start.15
  7.9 1.6 copy-start.11
  8.4 1.1 copy-start.5
  9.5 1.7 copy-start.3
  9.5 1.7 copy-start.7
  9.5 1.7 copy-start.9
  11.2 10.9 %collective-permute-start = (f32[256,896]{0,1:T(8,128)S(1)}, f32[256,896]{0,1:T(8,128)S(1)}, u32[]{:S(2)}, u32[]{:S(2)}) collective-permute-start(f32[256,896]{0,1:T(8,128)S(1)} %fusion), channel_id=1, source_target_pairs={{0,1},{1,0},{2,3},{3,2},{4,5},{5,4},{6,7},{7,6},{8,9},{9,8},{10,11... | collective-permute-start | bytes 2752520 | tf_op jit(solution)/shard_map/ppermute | solution.py:15
  22.2 23.5 %collective-permute-start.1 = (f32[256,896]{0,1:T(8,128)S(1)}, f32[256,896]{0,1:T(8,128)S(1)}, u32[]{:S(2)}, u32[]{:S(2)}) collective-permute-start(f32[256,896]{0,1:T(8,128)S(1)} %add.187), channel_id=1, source_target_pairs={{0,2},{1,3},{2,0},{3,1},{4,6},{5,7},{6,4},{7,5},{8,10},{9,11},{10,... | collective-permute-start | bytes 2752520 | tf_op jit(solution)/shard_map/ppermute | solution.py:15
  45.8 44.7 %collective-permute-start.2 = (f32[256,896]{0,1:T(8,128)S(1)}, f32[256,896]{0,1:T(8,128)S(1)}, u32[]{:S(2)}, u32[]{:S(2)}) collective-permute-start(f32[256,896]{0,1:T(8,128)S(1)} %add.188), channel_id=1, source_target_pairs={{0,4},{1,5},{2,6},{3,7},{4,0},{5,1},{6,2},{7,3},{8,12},{9,13},{10,... | collective-permute-start | bytes 2752520 | tf_op jit(solution)/shard_map/ppermute | solution.py:15
  90.6 47.1 %collective-permute-start.3 = (f32[256,896]{0,1:T(8,128)S(1)}, f32[256,896]{0,1:T(8,128)S(1)}, u32[]{:S(2)}, u32[]{:S(2)}) collective-permute-start(f32[256,896]{0,1:T(8,128)S(1)} %add.189), channel_id=1, source_target_pairs={{0,8},{1,9},{2,10},{3,11},{4,12},{5,13},{6,14},{7,15},{8,0},{9,1},... | collective-permute-start | bytes 2752520 | tf_op jit(solution)/shard_map/ppermute | solution.py:15
  137.8 23.3 %collective-permute-start.4 = (f32[256,896]{0,1:T(8,128)S(1)}, f32[256,896]{0,1:T(8,128)S(1)}, u32[]{:S(2)}, u32[]{:S(2)}) collective-permute-start(f32[256,896]{0,1:T(8,128)S(1)} %add.190), channel_id=1, source_target_pairs={{0,16},{1,17},{2,18},{3,19},{4,20},{5,21},{6,22},{7,23},{8,24},{9,... | collective-permute-start | bytes 2752520 | tf_op jit(solution)/shard_map/ppermute | solution.py:15
  161.2 23.9 %collective-permute-start.5 = (f32[256,896]{0,1:T(8,128)S(1)}, f32[256,896]{0,1:T(8,128)S(1)}, u32[]{:S(2)}, u32[]{:S(2)}) collective-permute-start(f32[256,896]{0,1:T(8,128)S(1)} %add.191), channel_id=1, source_target_pairs={{0,32},{1,33},{2,34},{3,35},{4,36},{5,37},{6,38},{7,39},{8,40},{9,... | collective-permute-start | bytes 2752520 | tf_op jit(solution)/shard_map/ppermute | solution.py:15
  185.2 21.6 %collective-permute-start.6 = (f32[256,896]{0,1:T(8,128)S(1)}, f32[256,896]{0,1:T(8,128)}, u32[]{:S(2)}, u32[]{:S(2)}) collective-permute-start(f32[256,896]{0,1:T(8,128)S(1)} %add.192), channel_id=1, source_target_pairs={{0,64},{1,65},{2,66},{3,67},{4,68},{5,69},{6,70},{7,71},{8,72},{9,... | collective-permute-start | bytes 2752520 | tf_op jit(solution)/shard_map/ppermute | solution.py:15
  270.7 1.3 copy-start.4
  272.0 1.3 copy-start.8
  272.0 1.3 copy-start.10
  273.3 1.0 copy-start.12
  275.6 6.8 collective-permute-start.7
  282.5 17.8 %collective-permute-start.8 = (f32[256,640]{0,1:T(8,128)S(1)}, f32[256,640]{0,1:T(8,128)S(1)}, u32[]{:S(2)}, u32[]{:S(2)}) collective-permute-start(f32[256,640]{0,1:T(8,128)S(1)} %add.195), channel_id=1, source_target_pairs={{0,2},{1,3},{2,0},{3,1},{4,6},{5,7},{6,4},{7,5},{8,10},{9,11},{10,... | collective-permute-start | bytes 1966088 | tf_op jit(solution)/shard_map/ppermute | solution.py:15
  300.4 33.4 %collective-permute-start.9 = (f32[256,640]{0,1:T(8,128)S(1)}, f32[256,640]{0,1:T(8,128)S(1)}, u32[]{:S(2)}, u32[]{:S(2)}) collective-permute-start(f32[256,640]{0,1:T(8,128)S(1)} %add.196), channel_id=1, source_target_pairs={{0,4},{1,5},{2,6},{3,7},{4,0},{5,1},{6,2},{7,3},{8,12},{9,13},{10,... | collective-permute-start | bytes 1966088 | tf_op jit(solution)/shard_map/ppermute | solution.py:15
  333.9 36.4 %collective-permute-start.10 = (f32[256,640]{0,1:T(8,128)S(1)}, f32[256,640]{0,1:T(8,128)S(1)}, u32[]{:S(2)}, u32[]{:S(2)}) collective-permute-start(f32[256,640]{0,1:T(8,128)S(1)} %add.197), channel_id=1, source_target_pairs={{0,8},{1,9},{2,10},{3,11},{4,12},{5,13},{6,14},{7,15},{8,0},{9,1},... | collective-permute-start | bytes 1966088 | tf_op jit(solution)/shard_map/ppermute | solution.py:15
  370.4 17.7 %collective-permute-start.11 = (f32[256,640]{0,1:T(8,128)S(1)}, f32[256,640]{0,1:T(8,128)S(1)}, u32[]{:S(2)}, u32[]{:S(2)}) collective-permute-start(f32[256,640]{0,1:T(8,128)S(1)} %add.198), channel_id=1, source_target_pairs={{0,16},{1,17},{2,18},{3,19},{4,20},{5,21},{6,22},{7,23},{8,24},{9,... | collective-permute-start | bytes 1966088 | tf_op jit(solution)/shard_map/ppermute | solution.py:15
  388.1 18.3 %collective-permute-start.12 = (f32[256,640]{0,1:T(8,128)S(1)}, f32[256,640]{0,1:T(8,128)S(1)}, u32[]{:S(2)}, u32[]{:S(2)}) collective-permute-start(f32[256,640]{0,1:T(8,128)S(1)} %add.199), channel_id=1, source_target_pairs={{0,32},{1,33},{2,34},{3,35},{4,36},{5,37},{6,38},{7,39},{8,40},{9,... | collective-permute-start | bytes 1966088 | tf_op jit(solution)/shard_map/ppermute | solution.py:15
  406.5 15.9 %collective-permute-start.13 = (f32[256,640]{0,1:T(8,128)S(1)}, f32[256,640]{0,1:T(8,128)S(1)}, u32[]{:S(2)}, u32[]{:S(2)}) collective-permute-start(f32[256,640]{0,1:T(8,128)S(1)} %add.200), channel_id=1, source_target_pairs={{0,64},{1,65},{2,66},{3,67},{4,68},{5,69},{6,70},{7,71},{8,72},{9,... | collective-permute-start | bytes 1966088 | tf_op jit(solution)/shard_map/ppermute | solution.py:15
  422.5 33.3 %collective-permute-start.14 = (f32[256,640]{0,1:T(8,128)S(1)}, f32[256,640]{0,1:T(8,128)}, u32[]{:S(2)}, u32[]{:S(2)}) collective-permute-start(f32[256,640]{0,1:T(8,128)S(1)} %add.201), channel_id=1, source_target_pairs={{0,128},{1,129},{2,130},{3,131},{4,132},{5,133},{6,134},{7,135},{8... | collective-permute-start | bytes 1966088 | tf_op jit(solution)/shard_map/ppermute | solution.py:15
  520.7 0.7 copy-start.13
  521.8 2.9 copy-start.14
  525.9 1.0 copy-start.6
  527.7 3.7 collective-permute-start.15
  531.5 12.2 %collective-permute-start.16 = (f32[256,384]{0,1:T(8,128)S(1)}, f32[256,384]{0,1:T(8,128)S(1)}, u32[]{:S(2)}, u32[]{:S(2)}) collective-permute-start(f32[256,384]{0,1:T(8,128)S(1)} %add.204), channel_id=1, source_target_pairs={{0,2},{1,3},{2,0},{3,1},{4,6},{5,7},{6,4},{7,5},{8,10},{9,11},{10,... | collective-permute-start | bytes 1179656 | tf_op jit(solution)/shard_map/ppermute | solution.py:15
  543.8 22.2 %collective-permute-start.17 = (f32[256,384]{0,1:T(8,128)S(1)}, f32[256,384]{0,1:T(8,128)S(1)}, u32[]{:S(2)}, u32[]{:S(2)}) collective-permute-start(f32[256,384]{0,1:T(8,128)S(1)} %add.205), channel_id=1, source_target_pairs={{0,4},{1,5},{2,6},{3,7},{4,0},{5,1},{6,2},{7,3},{8,12},{9,13},{10,... | collective-permute-start | bytes 1179656 | tf_op jit(solution)/shard_map/ppermute | solution.py:15
  566.1 24.6 %collective-permute-start.18 = (f32[256,384]{0,1:T(8,128)S(1)}, f32[256,384]{0,1:T(8,128)S(1)}, u32[]{:S(2)}, u32[]{:S(2)}) collective-permute-start(f32[256,384]{0,1:T(8,128)S(1)} %add.206), channel_id=1, source_target_pairs={{0,8},{1,9},{2,10},{3,11},{4,12},{5,13},{6,14},{7,15},{8,0},{9,1},... | collective-permute-start | bytes 1179656 | tf_op jit(solution)/shard_map/ppermute | solution.py:15
  590.7 12.1 %collective-permute-start.19 = (f32[256,384]{0,1:T(8,128)S(1)}, f32[256,384]{0,1:T(8,128)S(1)}, u32[]{:S(2)}, u32[]{:S(2)}) collective-permute-start(f32[256,384]{0,1:T(8,128)S(1)} %add.207), channel_id=1, source_target_pairs={{0,16},{1,17},{2,18},{3,19},{4,20},{5,21},{6,22},{7,23},{8,24},{9,... | collective-permute-start | bytes 1179656 | tf_op jit(solution)/shard_map/ppermute | solution.py:15
  602.8 12.7 %collective-permute-start.20 = (f32[256,384]{0,1:T(8,128)S(1)}, f32[256,384]{0,1:T(8,128)S(1)}, u32[]{:S(2)}, u32[]{:S(2)}) collective-permute-start(f32[256,384]{0,1:T(8,128)S(1)} %add.208), channel_id=1, source_target_pairs={{0,32},{1,33},{2,34},{3,35},{4,36},{5,37},{6,38},{7,39},{8,40},{9,... | collective-permute-start | bytes 1179656 | tf_op jit(solution)/shard_map/ppermute | solution.py:15
  615.6 10.2 %collective-permute-start.21 = (f32[256,384]{0,1:T(8,128)S(1)}, f32[256,384]{0,1:T(8,128)S(1)}, u32[]{:S(2)}, u32[]{:S(2)}) collective-permute-start(f32[256,384]{0,1:T(8,128)S(1)} %add.209), channel_id=1, source_target_pairs={{0,64},{1,65},{2,66},{3,67},{4,68},{5,69},{6,70},{7,71},{8,72},{9,... | collective-permute-start | bytes 1179656 | tf_op jit(solution)/shard_map/ppermute | solution.py:15
  625.9 22.2 %collective-permute-start.22 = (f32[256,384]{0,1:T(8,128)S(1)}, f32[256,384]{0,1:T(8,128)S(1)}, u32[]{:S(2)}, u32[]{:S(2)}) collective-permute-start(f32[256,384]{0,1:T(8,128)S(1)} %add.210), channel_id=1, source_target_pairs={{0,128},{1,129},{2,130},{3,131},{4,132},{5,133},{6,134},{7,135},{8... | collective-permute-start | bytes 1179656 | tf_op jit(solution)/shard_map/ppermute | solution.py:15
  648.2 21.5 %collective-permute-start.23 = (f32[256,384]{0,1:T(8,128)S(1)}, f32[256,384]{0,1:T(8,128)S(1)}, u32[]{:S(2)}, u32[]{:S(2)}) collective-permute-start(f32[256,384]{0,1:T(8,128)S(1)} %add.211), channel_id=1, source_target_pairs={{0,256},{1,257},{2,258},{3,259},{4,260},{5,261},{6,262},{7,263},{8... | collective-permute-start | bytes 1179656 | tf_op jit(solution)/shard_map/ppermute | solution.py:15
where the time goes:
time: 741 us; the launch traced here: 735 us
  waiting for transfers between devices  449 us (61%)
  other arithmetic  170 us (23%)
  starting transfers between devices  67 us (9%)
  local copies, waits for them, and re-layouts  22 us (3%)
  matrix products  19.3 us (3%)
    ppermute x24, waiting for transfers between devices, partner(): return lax.ppermute(value, axis, pairs)  449 us
    another operation x21, other arithmetic, on_device(): factor = jnp.linalg.cholesky(core)  104 us
    ppermute x24, starting transfers between devices, partner(): return lax.ppermute(value, axis, pairs)  67 us
    another operation x7, other arithmetic, on_device(): mixed = jax.scipy.linalg.cho_solve((factor, True), total[:, width:])  59.1 us
  transfers between devices with their start and end apart: 24, of which 24 were waited for; matrix products, arithmetic and copies ran while one was open for 0% of the time, Pallas kernels for 0%

commit v1 on v0

v1 whole, which is shorter than its diff:
```python
import math

import jax
import jax.numpy as jnp
import numpy as np
from jax import lax
from jax.experimental import pallas as pl
from jax.experimental.pallas import tpu as pltpu
from jax.sharding import PartitionSpec as P

PTS = 512
BLK = 128
WIDTH = 256
LEVELS = 3
KERNEL_GAIN = 64.0
TOP = 9
PAIRS = [
    [(i, j) for i, j in ((a, b) for a in (2 * l, 2 * l + 1) for b in range(a, 7))]
    for l in range(LEVELS)
]
COUNTS = [len(p) for p in PAIRS]
ROWS = [8 * c for c in COUNTS]
TOTAL = sum(ROWS)
NEWTON_LIMIT = 3.0e4
HIGHEST = lax.Precision.HIGHEST
VMEM = pl.BlockSpec(memory_space=pltpu.VMEM)
PARAMS = pltpu.CompilerParams(vmem_limit_bytes=48 * 2**20)


def dot(a, b, dims=((1,), (0,)), precision=HIGHEST):
    return lax.dot_general(a, b, (dims, ((), ())), precision=precision, preferred_element_type=jnp.float32)


def gram_kernel(noise_ref, feat_ref, targ_ref, anch_ref, gram_ref, panel_ref, scaled_ref):
    device = lax.axis_index("leaf")
    core = device & 1
    inverse = 1.0 / noise_ref[...]
    feats = feat_ref[...]
    wide = feats.astype(jnp.float32)
    point_norm = dot(jnp.ones((8, BLK), jnp.float32), wide * wide, ((1,), (1,)))[:1]
    for level in range(LEVELS):
        bit = TOP - LEVELS + level
        side = (device >> bit) & 1
        weight = KERNEL_GAIN / math.sqrt(PTS * 2 ** (bit + 1))
        for which in range(2):
            anchors = anch_ref[level, side ^ which]
            cross = dot(anchors, feats, ((1,), (1,)), None)
            a32 = anchors.astype(jnp.float32)
            anchor_norm = jnp.sum(a32 * a32, axis=1, keepdims=True)
            squared = point_norm + anchor_norm - 2.0 * cross
            scaled = jnp.sqrt(12.0 * jnp.maximum(squared, 0.0))
            values = weight * (1.0 + scaled) * jnp.exp(-scaled)
            at = BLK * (2 * level + which)
            panel_ref[at : at + BLK, :] = values
            scaled_ref[at : at + BLK, :] = values * inverse
    targets = targ_ref[...]
    place = 0
    for i in range(2 * LEVELS):
        left = panel_ref[BLK * i : BLK * (i + 1), :]
        right = scaled_ref[BLK * i :, :]
        products = dot(left, right, ((1,), (1,)))
        rhs = dot(scaled_ref[BLK * i : BLK * (i + 1), :], targets)
        for j in range(i, 7):
            block = rhs if j == 6 else products[:, BLK * (j - i) : BLK * (j - i + 1)]
            block = block.reshape(2, 8, 8, BLK)
            gram_ref[core, :, place : place + 8, :] = block[0]
            gram_ref[1 - core, :, place : place + 8, :] = block[1]
            place += 8


def gram(noise, features, targets, anchors):
    return pl.pallas_call(
        gram_kernel,
        out_shape=(
            jax.ShapeDtypeStruct((2, 8, TOTAL, BLK), jnp.float32),
            jax.ShapeDtypeStruct((2 * LEVELS * BLK, PTS), jnp.float32),
        ),
        in_specs=[VMEM] * 4,
        out_specs=(VMEM, VMEM),
        scratch_shapes=[pltpu.VMEM((2 * LEVELS * BLK, PTS), jnp.float32)],
        compiler_params=PARAMS,
    )(noise.reshape(1, PTS), features, targets, anchors)


def load_blocks(level, own_ref, other_ref, core, a_ref, b_ref):
    half = 64
    for k, (i, j) in enumerate(PAIRS[level]):
        row = BLK * (i - 2 * level)
        column = BLK * (j - 2 * level)
        dst, column = (a_ref, column) if column < WIDTH else (b_ref, column - WIDTH)
        for ref, which in ((own_ref, core), (other_ref, 1 - core)):
            at = pl.multiple_of(row + half * which, half)
            dst[pl.ds(at, half), column : column + BLK] = ref[:, 8 * k : 8 * k + 8, :].reshape(half, BLK)
    a_ref[BLK:, :BLK] = a_ref[:BLK, BLK:].T
    a_ref[...] = a_ref[...] + identity()


def identity():
    rows = lax.broadcasted_iota(jnp.int32, (WIDTH, WIDTH), 0)
    columns = lax.broadcasted_iota(jnp.int32, (WIDTH, WIDTH), 1)
    return jnp.where(rows == columns, 1.0, 0.0).astype(jnp.float32)


def invert(a_ref, x_ref):
    a = a_ref[...]
    bound = jnp.max(jnp.sum(jnp.abs(a), axis=0, keepdims=True))

    @pl.when(bound <= NEWTON_LIMIT)
    def _newton():
        low = 2.0 / (1.0 + bound)
        after = low * (2.0 - low)
        scale = 2.0 / (1.0 + after)
        x_ref[...] = (scale * low) * (2.0 * identity() - low * a)

        def more(state):
            return state[0] < 1.0 - 3e-7

        def step(state):
            low = state[0]
            after = low * (2.0 - low)
            scale = 2.0 / (1.0 + after)
            x = x_ref[...]
            rest = 2.0 * identity() - dot(a_ref[...], x)
            x_ref[...] = scale * dot(x, rest)
            return (scale * after,)

        lax.while_loop(more, step, (scale * after,))

    @pl.when(jnp.logical_not(bound <= NEWTON_LIMIT))
    def _direct():
        x_ref[...] = a
        lanes = lax.broadcasted_iota(jnp.int32, (1, WIDTH), 1)
        rows = lax.broadcasted_iota(jnp.int32, (WIDTH, 1), 0)

        def step(k, carry):
            x = x_ref[...]
            row = jnp.sum(jnp.where(rows == k, x, 0.0), axis=0, keepdims=True)
            column = jnp.sum(jnp.where(lanes == k, x, 0.0), axis=1, keepdims=True)
            pivot = jnp.sum(jnp.where(lanes == k, row, 0.0), axis=1, keepdims=True)
            row = jnp.where(lanes == k, 1.0, row) / pivot
            cleared = jnp.where(lanes == k, 0.0, x)
            x_ref[...] = jnp.where(rows == k, row, cleared - column * row)
            return carry

        lax.fori_loop(0, WIDTH, step, 0)


def level_kernel(level, own_ref, other_ref, rest_ref, coef_ref, new_ref, a_ref, x_ref, b_ref, t_ref):
    device = lax.axis_index("leaf")
    core = device & 1
    piece = 8 * core + 4 * ((device >> 6) & 1) + ((device >> 4) & 3)
    load_blocks(level, own_ref, other_ref, core, a_ref, b_ref)
    invert(a_ref, x_ref)
    coef_ref[...] = dot(x_ref[...], b_ref[...])
    blocks = 2 * (LEVELS - 1 - level)
    for k in range(blocks):
        t_ref[k * BLK : (k + 1) * BLK, :] = b_ref[:, k * BLK : (k + 1) * BLK].T
    mine = jnp.concatenate(
        [t_ref[pl.ds(pl.multiple_of(k * BLK + 8 * piece, 8), 8), :] for k in range(blocks)], axis=0
    )
    change = dot(mine, coef_ref[...])
    place = 0
    for later in range(level + 1, LEVELS):
        for i, j in PAIRS[later]:
            row = 8 * (i - 2 * (level + 1))
            column = BLK * (j - 2 * (level + 1))
            new_ref[place : place + 8, :] = (
                rest_ref[place : place + 8, :] - change[row : row + 8, column : column + BLK]
            )
            place += 8


def solve_level(level, own, other, rest):
    columns = WIDTH * (LEVELS - 1 - level) + BLK
    return pl.pallas_call(
        lambda *refs: level_kernel(level, *refs),
        out_shape=(
            jax.ShapeDtypeStruct((WIDTH, columns), jnp.float32),
            jax.ShapeDtypeStruct(rest.shape, jnp.float32),
        ),
        in_specs=[VMEM] * 3,
        out_specs=(VMEM, VMEM),
        scratch_shapes=[
            pltpu.VMEM((WIDTH, WIDTH), jnp.float32),
            pltpu.VMEM((WIDTH, WIDTH), jnp.float32),
            pltpu.VMEM((WIDTH, columns), jnp.float32),
            pltpu.VMEM((columns - BLK, WIDTH), jnp.float32),
        ],
        compiler_params=PARAMS,
    )(own, other, rest)


def split3(value):
    first = value.astype(jnp.bfloat16)
    left = value - first.astype(jnp.float32)
    second = left.astype(jnp.bfloat16)
    third = (left - second.astype(jnp.float32)).astype(jnp.bfloat16)
    return first, second, third


def as_column(row, k):
    return jnp.broadcast_to(row[:, BLK * k : BLK * (k + 1)], (BLK, BLK)).T


def last_kernel(
    own_ref, other_ref, coef0_ref, coef1_ref, panel_ref, noise_ref, targ_ref, order_ref,
    solved_ref, coupling_ref, a_ref, x_ref, b_ref, z_ref,
):
    device = lax.axis_index("leaf")
    core = device & 1
    load_blocks(LEVELS - 1, own_ref, other_ref, core, a_ref, b_ref)
    invert(a_ref, x_ref)
    z2 = dot(x_ref[...], b_ref[...])
    z1 = coef1_ref[:, WIDTH:] - dot(coef1_ref[:, :WIDTH], z2)
    z_ref[WIDTH : 2 * WIDTH, :] = z1
    z_ref[2 * WIDTH :, :] = z2
    z0 = coef0_ref[:, 2 * WIDTH :] - dot(coef0_ref[:, : 2 * WIDTH], z_ref[WIDTH:, :])
    z_ref[:WIDTH, :] = z0
    coupling_ref[0] = coef0_ref[:, 2 * WIDTH :]
    coupling_ref[1] = coef1_ref[:, WIDTH:]
    coupling_ref[2] = z2
    left = targ_ref[...] - dot(panel_ref[...], z_ref[...], ((0,), (0,)))
    inverse = 1.0 / noise_ref[...]
    local = order_ref[...] - device * PTS
    left = left * jnp.concatenate([as_column(inverse, k) for k in range(4)], axis=0)
    pieces = jnp.concatenate(split3(left), axis=1)
    lanes = lax.broadcasted_iota(jnp.int32, (BLK, PTS), 1).astype(jnp.float32)
    for k in range(4):
        wanted = as_column(local.astype(jnp.float32), k)
        wanted = jnp.concatenate([wanted] * 4, axis=1)
        pick = jnp.where(wanted == lanes, 1.0, 0.0).astype(jnp.bfloat16)
        moved = dot(pick, pieces, precision=None)
        solved_ref[BLK * k : BLK * (k + 1), :] = (moved[:, :BLK] + moved[:, BLK : 2 * BLK]) + moved[:, 2 * BLK :]


def solve_last(own, other, coef0, coef1, panel, noise, targets, order):
    return pl.pallas_call(
        last_kernel,
        out_shape=(
            jax.ShapeDtypeStruct((PTS, BLK), jnp.float32),
            jax.ShapeDtypeStruct((LEVELS, WIDTH, BLK), jnp.float32),
        ),
        in_specs=[VMEM] * 8,
        out_specs=(VMEM, VMEM),
        scratch_shapes=[
            pltpu.VMEM((WIDTH, WIDTH), jnp.float32),
            pltpu.VMEM((WIDTH, WIDTH), jnp.float32),
            pltpu.VMEM((WIDTH, BLK), jnp.float32),
            pltpu.VMEM((LEVELS * WIDTH, BLK), jnp.float32),
        ],
        compiler_params=PARAMS,
    )(own, other, coef0, coef1, panel, noise.reshape(1, PTS), targets, order.reshape(1, PTS))


GRID = np.arange(512).reshape(4, 2, 4, 8, 2)
PLANE = GRID.transpose(0, 3, 4, 1, 2).reshape(-1, 8).tolist()


def partner(value, bit):
    return lax.ppermute(value, "leaf", [(i, i ^ (1 << bit)) for i in range(512)])


def exchange(value):
    return lax.all_to_all(value, "leaf", 0, 0, axis_index_groups=PLANE)


def gather_rows(rows):
    own = exchange(jnp.broadcast_to(rows[None], (8, *rows.shape)))
    return own, partner(own, 0)


def on_device(features, noise, targets, anchors, order):
    both, panel = gram(noise, features, targets, anchors)
    half = both[0] + partner(both[1], 0)
    rows = jnp.sum(exchange(half), axis=0)
    for bit in (1, 2, 3):
        rows = rows + partner(rows, bit)
    own, other = gather_rows(rows[: ROWS[0]])
    coef0, rest = solve_level(0, own, other, rows[ROWS[0] :])
    rest = rest + partner(rest, 7)
    own, other = gather_rows(rest[: ROWS[1]])
    coef1, rest = solve_level(1, own, other, rest[ROWS[1] :])
    rest = rest + partner(rest, 8)
    own, other = gather_rows(rest)
    return solve_last(own, other, coef0, coef1, panel, noise, targets, order)


def solution(mesh):
    in_specs = (P("leaf", None), P("leaf"), P("leaf", None), P(), P("leaf"))
    out_specs = (P("leaf", None), P(None, "leaf", None))
    return jax.shard_map(on_device, mesh=mesh, in_specs=in_specs, out_specs=out_specs, check_vma=False)
```

time: 741 us -> 150 us (0.20)
  waiting for transfers between devices: 449 us -> 21.8 us
  other arithmetic: 170 us -> 0.19 us
  blocking collectives: 0 us -> 45.4 us
  Pallas kernels: 0 us -> 31.3 us
  starting transfers between devices: 67 us -> 46.5 us
  matrix products: 19.3 us -> 0 us
  local copies, waits for them, and re-layouts: 22 us -> 3.61 us
    ppermute x24 -> x9, waiting for transfers between devices: 449 us -> 21.8 us  [partner(): return lax.ppermute(value, 'leaf', [(i, i ^ 1 << bit) for i in range(512)])]
    another operation x32 -> x0, other arithmetic: 164 us -> none  [the longest x21 104 us: on_device(): factor = jnp.linalg.cholesky(core)]
    all_to_all x0 -> x4, blocking collectives: none -> 45.4 us  [exchange(): return lax.all_to_all(value, 'leaf', 0, 0, axis_index_groups=PLANE)]
    pallas_call x0 -> x4, Pallas kernels: none -> 31.3 us  [the longest x2 15.1 us: solve_level(): pl.pallas_call(lambda *refs: level_kernel(level, *refs), out_shape=(jax.S...]
    ppermute x24 -> x9, starting transfers between devices: 67 us -> 46.5 us  [partner(): return lax.ppermute(value, 'leaf', [(i, i ^ 1 << bit) for i in range(512)])]
    another operation x25 -> x0, local copies, waits for them, and re-layouts: 12.7 us -> none
    another operation x24 -> x0, matrix products: 11.7 us -> none  [the longest x18 8.57 us: on_device(): mixed = jax.scipy.linalg.cho_solve((factor, True), total[:, width:])]
    dot_general x9 -> x0, matrix products: 7.64 us -> none  [the longest x3 3.69 us: on_device(): lax.dot_general(panels[level], stack, (((0,), (0,)), ((), ())), precision...]
  transfers between devices with their start and end apart: 24 -> 9, of which waited for: 24 -> 9; matrix products, arithmetic and copies ran while one was open for 0% -> 0% of each run, Pallas kernels for 0% -> 0%
where the time goes in v1:
time: 150 us
  starting transfers between devices  46.5 us (31%)
  blocking collectives  45.4 us (30%)
  Pallas kernels  31.3 us (21%)
  waiting for transfers between devices  21.8 us (15%)
  local copies, waits for them, and re-layouts  3.61 us (2%)
    ppermute x9, starting transfers between devices, partner(): return lax.ppermute(value, 'leaf', [(i, i ^ 1 << bit) for i in range(512)])  46.5 us
    all_to_all x4, blocking collectives, exchange(): return lax.all_to_all(value, 'leaf', 0, 0, axis_index_groups=PLANE)  45.4 us
    ppermute x9, waiting for transfers between devices, partner(): return lax.ppermute(value, 'leaf', [(i, i ^ 1 << bit) for i in range(512)])  21.8 us
    pallas_call x2, Pallas kernels, solve_level(): pl.pallas_call(lambda *refs: level_kernel(level, *refs), out_shape=(jax.S...  15.1 us
    pallas_call x1, Pallas kernels, solve_last(): pl.pallas_call(last_kernel, out_shape=(jax.ShapeDtypeStruct((PTS, BLK), j...  9.1 us
    pallas_call x1, Pallas kernels, gram(): pl.pallas_call(gram_kernel, out_shape=(jax.ShapeDtypeStruct((2, 8, TOTAL,...  7.12 us
    unnamed x14, local copies, waits for them, and re-layouts  3.47 us
  transfers between devices with their start and end apart: 9, of which 9 were waited for; matrix products, arithmetic and copies ran while one was open for 0% of the time, Pallas kernels for 0%

profile of v1, /device:TPU:1, one launch (start us, length us, event | category | flops | bytes accessed | tf_op | source)
XLA Modules:
  0.0 149.6 jit_solution(227077104780085880)
XLA Ops:
  0.6 0.0 copy-start
  0.6 0.9 copy-done
  1.6 0.0 copy-start.2
  1.6 0.9 copy-done.2
  2.5 0.0 copy-start.3
  2.5 0.9 copy-done.3
  3.4 0.0 copy-start.4
  3.4 0.7 copy-done.4
  4.1 7.1 %shard_map.68 = (f32[2,8,216,128]{3,2,1,0:T(8,128)S(1)}, f32[768,512]{1,0:T(8,128)S(1)}) custom-call(f32[1,512]{1,0:T(1,128)S(1)} %bitcast.6, bf16[512,128]{1,0:T(8,128)(2,1)S(1)} %copy-done.3, f32[512,128]{1,0:T(8,128)S(1)} %copy-done, bf16[3,2,128,128]{3,2,1,0:T(8,128)(2,1)S(1)} %copy-done.2), custom_call_target="tpu_custom_call" | custom-call | tf_op jit(solution)/shard_map/pallas_call | solution.py:72
  11.2 0.1 slice_bitcast_fusion
  11.3 8.8 %collective-permute-start = (f32[8,216,128]{2,1,0:T(8,128)S(1)}, f32[8,216,128]{2,1,0:T(8,128)S(1)}, u32[]{:S(2)}, u32[]{:S(2)}) collective-permute-start(f32[8,216,128]{2,1,0:T(8,128)S(1)} %slice_bitcast_fusion), channel_id=1, source_target_pairs={{0,1},{1,0},{2,3},{3,2},{4,5},{5,4},{6,7},{7,6},{8,9},{9,8},{10,11... | collective-permute-start | bytes 2654216 | tf_op jit(solution)/shard_map/ppermute | solution.py:260
  20.1 2.0 %collective-permute-done = f32[8,216,128]{2,1,0:T(8,128)S(1)} collective-permute-done((f32[8,216,128]{2,1,0:T(8,128)S(1)}, f32[8,216,128]{2,1,0:T(8,128)S(1)}, u32[]{:S(2)}, u32[]{:S(2)}) %collective-permute-start) | collective-permute-done | bytes 884768 | tf_op jit(solution)/shard_map/ppermute | solution.py:260
  22.1 0.1 bitcast_add_fusion
  22.2 15.8 %all_to_all.20 = f32[8,216,128]{2,1,0:T(8,128)S(1)} all-to-all(f32[8,216,128]{2,1,0:T(8,128)S(1)} %bitcast_add_fusion), channel_id=1, replica_groups={{0,16,32,48,64,80,96,112},{1,17,33,49,65,81,97,113},{2,18,34,50,66,82,9..., dimensions={0} | all-to-all | bytes 1769472 | tf_op jit(solution)/shard_map/all_to_all | solution.py:264
  38.1 1.9 %collective-permute-start.1 = (f32[216,128]{1,0:T(8,128)S(1)}, f32[216,128]{1,0:T(8,128)S(1)}, u32[]{:S(2)}, u32[]{:S(2)}) collective-permute-start(f32[216,128]{1,0:T(8,128)S(1)} %reduce_sum.9), channel_id=1, source_target_pairs={{0,2},{1,3},{2,0},{3,1},{4,6},{5,7},{6,4},{7,5},{8,10},{9,11},{10,... | collective-permute-start | bytes 331784 | tf_op jit(solution)/shard_map/ppermute | solution.py:260
  40.0 3.6 %collective-permute-done.1 = f32[216,128]{1,0:T(8,128)S(1)} collective-permute-done((f32[216,128]{1,0:T(8,128)S(1)}, f32[216,128]{1,0:T(8,128)S(1)}, u32[]{:S(2)}, u32[]{:S(2)}) %collective-permute-start.1) | collective-permute-done | bytes 110624 | tf_op jit(solution)/shard_map/ppermute | solution.py:260
  43.6 3.2 %collective-permute-start.2 = (f32[216,128]{1,0:T(8,128)S(1)}, f32[216,128]{1,0:T(8,128)S(1)}, u32[]{:S(2)}, u32[]{:S(2)}) collective-permute-start(f32[216,128]{1,0:T(8,128)S(1)} %add.19), channel_id=1, source_target_pairs={{0,4},{1,5},{2,6},{3,7},{4,0},{5,1},{6,2},{7,3},{8,12},{9,13},{10,... | collective-permute-start | bytes 331784 | tf_op jit(solution)/shard_map/ppermute | solution.py:260
  46.8 4.4 %collective-permute-done.2 = f32[216,128]{1,0:T(8,128)S(1)} collective-permute-done((f32[216,128]{1,0:T(8,128)S(1)}, f32[216,128]{1,0:T(8,128)S(1)}, u32[]{:S(2)}, u32[]{:S(2)}) %collective-permute-start.2) | collective-permute-done | bytes 110624 | tf_op jit(solution)/shard_map/ppermute | solution.py:260
  51.2 7.4 %collective-permute-start.3 = (f32[216,128]{1,0:T(8,128)S(1)}, f32[216,128]{1,0:T(8,128)S(1)}, u32[]{:S(2)}, u32[]{:S(2)}) collective-permute-start(f32[216,128]{1,0:T(8,128)S(1)} %add.20), channel_id=1, source_target_pairs={{0,8},{1,9},{2,10},{3,11},{4,12},{5,13},{6,14},{7,15},{8,0},{9,1},... | collective-permute-start | bytes 331784 | tf_op jit(solution)/shard_map/ppermute | solution.py:260
  58.6 2.3 %collective-permute-done.3 = f32[216,128]{1,0:T(8,128)S(1)} collective-permute-done((f32[216,128]{1,0:T(8,128)S(1)}, f32[216,128]{1,0:T(8,128)S(1)}, u32[]{:S(2)}, u32[]{:S(2)}) %collective-permute-start.3) | collective-permute-done | bytes 110624 | tf_op jit(solution)/shard_map/ppermute | solution.py:260
  61.0 11.9 %all_to_all.21.refs_0_ = f32[8,104,128]{2,1,0:T(8,128)S(1)} all-to-all(f32[8,104,128]{2,1,0:T(8,128)S(1)} %broadcast_in_dim.6), channel_id=1, replica_groups={{0,16,32,48,64,80,96,112},{1,17,33,49,65,81,97,113},{2,18,34,50,66,82,9..., dimensions={0} | all-to-all | bytes 851968 | tf_op jit(solution)/shard_map/all_to_all | solution.py:264
  72.9 0.0 copy-start.1
  72.9 0.0 copy-start.5
  72.9 0.0 copy-start.6
  72.9 7.0 %collective-permute-start.4 = (f32[8,104,128]{2,1,0:T(8,128)S(1)}, f32[8,104,128]{2,1,0:T(8,128)S(1)}, u32[]{:S(2)}, u32[]{:S(2)}) collective-permute-start(f32[8,104,128]{2,1,0:T(8,128)S(1)} %all_to_all.21.refs_0_), channel_id=1, source_target_pairs={{0,1},{1,0},{2,3},{3,2},{4,5},{5,4},{6,7},{7,6},{8,9},{9,8},{10,11... | collective-permute-start | bytes 1277960 | tf_op jit(solution)/shard_map/ppermute | solution.py:260
  79.9 1.4 collective-permute-done.4.refs_1_
  81.3 10.4 %shard_map.69 = (f32[256,640]{1,0:T(8,128)S(1)}, f32[112,128]{1,0:T(8,128)S(1)}) custom-call(f32[8,104,128]{2,1,0:T(8,128)S(1)} %all_to_all.21.refs_0_, f32[8,104,128]{2,1,0:T(8,128)S(1)} %collective-permute-done.4.refs_1_, f32[112,128]{1,0:T(8,128)S(1)} %slice.25.refs_2_), custom_call_target="tpu_custom_call" | custom-call | tf_op jit(solution)/shard_map/pallas_call | solution.py:175
  91.7 3.9 %collective-permute-start.5 = (f32[112,128]{1,0:T(8,128)S(1)}, f32[112,128]{1,0:T(8,128)S(1)}, u32[]{:S(2)}, u32[]{:S(2)}) collective-permute-start(f32[112,128]{1,0:T(8,128)S(1)} %get-tuple-element.9), channel_id=1, source_target_pairs={{0,128},{1,129},{2,130},{3,131},{4,132},{5,133},{6,134},{7,135},{8... | collective-permute-start | bytes 172040 | tf_op jit(solution)/shard_map/ppermute | solution.py:260
  95.6 3.8 %collective-permute-done.5 = f32[112,128]{1,0:T(8,128)S(1)} collective-permute-done((f32[112,128]{1,0:T(8,128)S(1)}, f32[112,128]{1,0:T(8,128)S(1)}, u32[]{:S(2)}, u32[]{:S(2)}) %collective-permute-start.5) | collective-permute-done | bytes 57376 | tf_op jit(solution)/shard_map/ppermute | solution.py:260
  99.5 9.6 %all_to_all.22.refs_0_ = f32[8,72,128]{2,1,0:T(8,128)S(1)} all-to-all(f32[8,72,128]{2,1,0:T(8,128)S(1)} %broadcast_in_dim.7), channel_id=1, replica_groups={{0,16,32,48,64,80,96,112},{1,17,33,49,65,81,97,113},{2,18,34,50,66,82,9..., dimensions={0} | all-to-all | bytes 589824 | tf_op jit(solution)/shard_map/all_to_all | solution.py:264
  109.1 3.5 %collective-permute-start.6 = (f32[8,72,128]{2,1,0:T(8,128)S(1)}, f32[8,72,128]{2,1,0:T(8,128)S(1)}, u32[]{:S(2)}, u32[]{:S(2)}) collective-permute-start(f32[8,72,128]{2,1,0:T(8,128)S(1)} %all_to_all.22.refs_0_), channel_id=1, source_target_pairs={{0,1},{1,0},{2,3},{3,2},{4,5},{5,4},{6,7},{7,6},{8,9},{9,8},{10,11... | collective-permute-start | bytes 884744 | tf_op jit(solution)/shard_map/ppermute | solution.py:260
  112.6 1.2 collective-permute-done.6.refs_1_
  113.8 4.7 %shard_map.70 = (f32[256,384]{1,0:T(8,128)S(1)}, f32[40,128]{1,0:T(8,128)S(1)}) custom-call(f32[8,72,128]{2,1,0:T(8,128)S(1)} %all_to_all.22.refs_0_, f32[8,72,128]{2,1,0:T(8,128)S(1)} %collective-permute-done.6.refs_1_, f32[40,128]{1,0:T(8,128)S(1)} %slice.27.refs_2_), custom_call_target="tpu_custom_call" | custom-call | tf_op jit(solution)/shard_map/pallas_call | solution.py:175
  118.5 6.2 %collective-permute-start.7 = (f32[40,128]{1,0:T(8,128)S(1)}, f32[40,128]{1,0:T(8,128)S(1)}, u32[]{:S(2)}, u32[]{:S(2)}) collective-permute-start(f32[40,128]{1,0:T(8,128)S(1)} %get-tuple-element.10), channel_id=1, source_target_pairs={{0,256},{1,257},{2,258},{3,259},{4,260},{5,261},{6,262},{7,263},{8... | collective-permute-start | bytes 61448 | tf_op jit(solution)/shard_map/ppermute | solution.py:260
  124.7 2.2 %collective-permute-done.7 = f32[40,128]{1,0:T(8,128)S(1)} collective-permute-done((f32[40,128]{1,0:T(8,128)S(1)}, f32[40,128]{1,0:T(8,128)S(1)}, u32[]{:S(2)}, u32[]{:S(2)}) %collective-permute-start.7) | collective-permute-done | bytes 20512 | tf_op jit(solution)/shard_map/ppermute | solution.py:260
  126.9 8.0 %all_to_all.23.own_ref = f32[8,40,128]{2,1,0:T(8,128)S(1)} all-to-all(f32[8,40,128]{2,1,0:T(8,128)S(1)} %broadcast_in_dim.8), channel_id=1, replica_groups={{0,16,32,48,64,80,96,112},{1,17,33,49,65,81,97,113},{2,18,34,50,66,82,9..., dimensions={0} | all-to-all | bytes 327680 | tf_op jit(solution)/shard_map/all_to_all | solution.py:264
  134.9 4.6 %collective-permute-start.8 = (f32[8,40,128]{2,1,0:T(8,128)S(1)}, f32[8,40,128]{2,1,0:T(8,128)S(1)}, u32[]{:S(2)}, u32[]{:S(2)}) collective-permute-start(f32[8,40,128]{2,1,0:T(8,128)S(1)} %all_to_all.23.own_ref), channel_id=1, source_target_pairs={{0,1},{1,0},{2,3},{3,2},{4,5},{5,4},{6,7},{7,6},{8,9},{9,8},{10,11... | collective-permute-start | bytes 491528 | tf_op jit(solution)/shard_map/ppermute | solution.py:260
  139.5 1.0 collective-permute-done.8.other_ref
  140.5 0.0 copy-done.1
  140.5 0.0 copy-done.5
  140.5 0.0 copy-done.6
  140.5 9.1 %shard_map.71 = (f32[512,128]{1,0:T(8,128)}, f32[3,256,128]{2,1,0:T(8,128)}) custom-call(f32[8,40,128]{2,1,0:T(8,128)S(1)} %all_to_all.23.own_ref, f32[8,40,128]{2,1,0:T(8,128)S(1)} %collective-permute-done.8.other_ref, f32[256,640]{1,0:T(8,128)S(1)} %get-tuple-element.11.coef0_ref, f32[256,384]{1,0:T(8,128)S(1)} %get-tuple-element.12.coef1_ref, ...), custom_call_target="tpu_custom_call" | custom-call | tf_op jit(solution)/shard_map/pallas_call | solution.py:237
  (13 shorter events, 0.2 us)
Async XLA Ops:
  0.6 1.0 copy-start
  1.6 0.9 copy-start.2
  2.5 0.9 copy-start.3
  3.4 0.7 copy-start.4
  11.3 10.8 %collective-permute-start = (f32[8,216,128]{2,1,0:T(8,128)S(1)}, f32[8,216,128]{2,1,0:T(8,128)S(1)}, u32[]{:S(2)}, u32[]{:S(2)}) collective-permute-start(f32[8,216,128]{2,1,0:T(8,128)S(1)} %slice_bitcast_fusion), channel_id=1, source_target_pairs={{0,1},{1,0},{2,3},{3,2},{4,5},{5,4},{6,7},{7,6},{8,9},{9,8},{10,11... | collective-permute-start | bytes 2654216 | tf_op jit(solution)/shard_map/ppermute | solution.py:260
  38.1 5.5 %collective-permute-start.1 = (f32[216,128]{1,0:T(8,128)S(1)}, f32[216,128]{1,0:T(8,128)S(1)}, u32[]{:S(2)}, u32[]{:S(2)}) collective-permute-start(f32[216,128]{1,0:T(8,128)S(1)} %reduce_sum.9), channel_id=1, source_target_pairs={{0,2},{1,3},{2,0},{3,1},{4,6},{5,7},{6,4},{7,5},{8,10},{9,11},{10,... | collective-permute-start | bytes 331784 | tf_op jit(solution)/shard_map/ppermute | solution.py:260
  43.6 7.6 %collective-permute-start.2 = (f32[216,128]{1,0:T(8,128)S(1)}, f32[216,128]{1,0:T(8,128)S(1)}, u32[]{:S(2)}, u32[]{:S(2)}) collective-permute-start(f32[216,128]{1,0:T(8,128)S(1)} %add.19), channel_id=1, source_target_pairs={{0,4},{1,5},{2,6},{3,7},{4,0},{5,1},{6,2},{7,3},{8,12},{9,13},{10,... | collective-permute-start | bytes 331784 | tf_op jit(solution)/shard_map/ppermute | solution.py:260
  51.2 9.7 %collective-permute-start.3 = (f32[216,128]{1,0:T(8,128)S(1)}, f32[216,128]{1,0:T(8,128)S(1)}, u32[]{:S(2)}, u32[]{:S(2)}) collective-permute-start(f32[216,128]{1,0:T(8,128)S(1)} %add.20), channel_id=1, source_target_pairs={{0,8},{1,9},{2,10},{3,11},{4,12},{5,13},{6,14},{7,15},{8,0},{9,1},... | collective-permute-start | bytes 331784 | tf_op jit(solution)/shard_map/ppermute | solution.py:260
  72.9 67.6 %copy-start.1 = (f32[512,128]{1,0:T(8,128)S(1)}, f32[512,128]{1,0:T(8,128)}, u32[]{:S(2)}) copy-start(f32[512,128]{1,0:T(8,128)} %targ_ref.3) | copy-start | bytes 786436
  72.9 67.6 %copy-start.5 = (f32[512]{0:T(512)S(1)}, f32[512]{0:T(512)}, u32[]{:S(2)}) copy-start(f32[512]{0:T(512)} %param.6) | copy-start | bytes 6148
  72.9 67.6 %copy-start.6 = (s32[512]{0:T(512)S(1)}, s32[512]{0:T(512)}, u32[]{:S(2)}) copy-start(s32[512]{0:T(512)} %param.9) | copy-start | bytes 6148
  72.9 8.4 %collective-permute-start.4 = (f32[8,104,128]{2,1,0:T(8,128)S(1)}, f32[8,104,128]{2,1,0:T(8,128)S(1)}, u32[]{:S(2)}, u32[]{:S(2)}) collective-permute-start(f32[8,104,128]{2,1,0:T(8,128)S(1)} %all_to_all.21.refs_0_), channel_id=1, source_target_pairs={{0,1},{1,0},{2,3},{3,2},{4,5},{5,4},{6,7},{7,6},{8,9},{9,8},{10,11... | collective-permute-start | bytes 1277960 | tf_op jit(solution)/shard_map/ppermute | solution.py:260
  91.7 7.7 %collective-permute-start.5 = (f32[112,128]{1,0:T(8,128)S(1)}, f32[112,128]{1,0:T(8,128)S(1)}, u32[]{:S(2)}, u32[]{:S(2)}) collective-permute-start(f32[112,128]{1,0:T(8,128)S(1)} %get-tuple-element.9), channel_id=1, source_target_pairs={{0,128},{1,129},{2,130},{3,131},{4,132},{5,133},{6,134},{7,135},{8... | collective-permute-start | bytes 172040 | tf_op jit(solution)/shard_map/ppermute | solution.py:260
  109.1 4.7 %collective-permute-start.6 = (f32[8,72,128]{2,1,0:T(8,128)S(1)}, f32[8,72,128]{2,1,0:T(8,128)S(1)}, u32[]{:S(2)}, u32[]{:S(2)}) collective-permute-start(f32[8,72,128]{2,1,0:T(8,128)S(1)} %all_to_all.22.refs_0_), channel_id=1, source_target_pairs={{0,1},{1,0},{2,3},{3,2},{4,5},{5,4},{6,7},{7,6},{8,9},{9,8},{10,11... | collective-permute-start | bytes 884744 | tf_op jit(solution)/shard_map/ppermute | solution.py:260
  118.5 8.4 %collective-permute-start.7 = (f32[40,128]{1,0:T(8,128)S(1)}, f32[40,128]{1,0:T(8,128)S(1)}, u32[]{:S(2)}, u32[]{:S(2)}) collective-permute-start(f32[40,128]{1,0:T(8,128)S(1)} %get-tuple-element.10), channel_id=1, source_target_pairs={{0,256},{1,257},{2,258},{3,259},{4,260},{5,261},{6,262},{7,263},{8... | collective-permute-start | bytes 61448 | tf_op jit(solution)/shard_map/ppermute | solution.py:260
  134.9 5.6 %collective-permute-start.8 = (f32[8,40,128]{2,1,0:T(8,128)S(1)}, f32[8,40,128]{2,1,0:T(8,128)S(1)}, u32[]{:S(2)}, u32[]{:S(2)}) collective-permute-start(f32[8,40,128]{2,1,0:T(8,128)S(1)} %all_to_all.23.own_ref), channel_id=1, source_target_pairs={{0,1},{1,0},{2,3},{3,2},{4,5},{5,4},{6,7},{7,6},{8,9},{9,8},{10,11... | collective-permute-start | bytes 491528 | tf_op jit(solution)/shard_map/ppermute | solution.py:260
